TPU v7x, 32 devices: a whole 2x2x4 slice. The times are simulated.
32 devices in a mesh: gx: 4 (over x, core), gy: 8 (over z, y).
Axes of the slice: x: 2, y: 2, z: 4, core: 2. Of those that a mesh axis runs over, the one named last changes fastest.
Arguments:
- nest_state: float32 [4, 8, 96, 3072], P(None, None, 'gx', 'gy'), may hold values from -6 to 6
- parent_state: float32 [4, 8, 96, 3072], P(None, None, 'gx', 'gy'), may hold values from -6 to 6
- offset_x: int32 [1], replicated, may hold values from 1 to 15
- offset_y: int32 [1], replicated, may hold values from 385 to 511
Outputs:
- nest_out: float32 [4, 8, 96, 3072], P(None, None, 'gx', 'gy')
- parent_out: float32 [4, 8, 96, 3072], P(None, None, 'gx', 'gy')
All inputs are finite; a program needn't handle non-finite values.
Results may differ from a plain program's by a relative error of at most 0.00019.
Values sent between devices are 32-bit elements; how exact they have to be, the bound alone decides.
A program may use at most 128 MiB of HBM per device.

v0:
```python
import jax
import jax.numpy as jnp
from jax import lax
from jax.sharding import PartitionSpec as P

SUBSTEPS = 3
CARRY_RATE = 0.35
SOUND_RATE = 0.4
MIXING_RATE = 0.2


def extended(value, sides, width):
    for axis, dim in sides:
        size, length = (lax.axis_size(axis), value.shape[dim])
        up = [(i, (i + 1) % size) for i in range(size - 1)]
        down = [(j, i) for i, j in up]
        last = lax.slice_in_dim(value, length - width, length, axis=dim)
        initial = lax.slice_in_dim(value, 0, width, axis=dim)
        before = lax.ppermute(last, axis, up)
        after = lax.ppermute(initial, axis, down)
        value = jnp.concatenate([before, value, after], axis=dim)
    return value


def advance(padded):
    center = padded[:, :, 1:-1, 1:-1]
    slope_x = (padded[:, :, 2:, 1:-1] - padded[:, :, :-2, 1:-1]) * 0.5
    slope_y = (padded[:, :, 1:-1, 2:] - padded[:, :, 1:-1, :-2]) * 0.5
    carried = center[0][None] * slope_x[:3] + center[1][None] * slope_y[:3]
    potential = center[2]
    level_above = jnp.concatenate([potential[1:], potential[-1:]], axis=0)
    level_below = jnp.concatenate([potential[:1], potential[:-1]], axis=0)
    wind_east = center[0] - CARRY_RATE * carried[0] - SOUND_RATE * slope_x[3]
    wind_north = center[1] - CARRY_RATE * carried[1] - SOUND_RATE * slope_y[3]
    heat_next = (
        potential
        - CARRY_RATE * carried[2]
        + MIXING_RATE * (level_above - 2.0 * potential + level_below)
    )
    pressure = center[3] - SOUND_RATE * (slope_x[0] + slope_y[1])
    return jnp.stack([wind_east, wind_north, heat_next, pressure])


def place_along(piece, first, width, axis):
    length = piece.shape[axis]
    target = lax.broadcasted_iota(jnp.int32, (length, width), 0) - first
    places = lax.broadcasted_iota(jnp.int32, (length, width), 1)
    table = (target == places).astype(jnp.float32)
    moved = jnp.moveaxis(piece, axis, -1)
    placed = jnp.dot(
        moved, table, precision=lax.Precision.HIGHEST, preferred_element_type=jnp.float32
    )
    return jnp.moveaxis(placed, -1, axis)


def on_device(nest_state, parent_state, offset_x, offset_y):
    shift_x = offset_x[0]
    shift_y = offset_y[0]
    count_x = lax.axis_size("gx")
    count_y = lax.axis_size("gy")
    index_x = lax.axis_index("gx")
    index_y = lax.axis_index("gy")
    levels = nest_state.shape[1]
    nest_cols = nest_state.shape[2]
    nest_rows = nest_state.shape[3]
    parent_cols = parent_state.shape[2]
    parent_rows = parent_state.shape[3]
    coarse_cols = nest_cols // 3
    coarse_rows = nest_rows // 3
    span_x = count_x * coarse_cols
    span_y = count_y * coarse_rows

    def take_slab(wanted, owner_index, extent, axis):
        local = wanted - owner_index * extent
        inside = (local >= 0) & (local < extent)
        slab = lax.dynamic_slice_in_dim(parent_state, jnp.clip(local, 0, extent - 1), 1, axis)
        return jnp.where(inside, jnp.squeeze(slab, axis), 0.0)

    columns = jnp.stack(
        [
            take_slab(shift_x - 1, index_x, parent_cols, 2),
            take_slab(shift_x + span_x, index_x, parent_cols, 2),
        ]
    )
    columns = lax.psum(columns, "gx")
    row_pair = jnp.stack(
        [
            take_slab(shift_y - 1, index_y, parent_rows, 3),
            take_slab(shift_y + span_y, index_y, parent_rows, 3),
        ]
    )
    row_pair = lax.psum(row_pair, "gy")
    column_first = shift_y + index_y * coarse_rows - 1
    row_first = shift_x + index_x * coarse_cols - 1
    column_strip = place_along(
        lax.all_gather(columns, "gy", axis=3, tiled=True), column_first, coarse_rows + 2, 3
    )
    row_strip = place_along(
        lax.all_gather(row_pair, "gx", axis=3, tiled=True), row_first, coarse_cols + 2, 3
    )
    column_strip = jnp.repeat(column_strip, 3, axis=3)
    row_strip = jnp.repeat(row_strip, 3, axis=3)
    parent_padded = extended(parent_state, (("gx", 2), ("gy", 3)), 1)
    parent_next = advance(parent_padded)
    fields = nest_state
    for substep in range(SUBSTEPS):
        padded = extended(fields, (("gx", 2), ("gy", 3)), 1)
        col_pos = lax.broadcasted_iota(jnp.int32, (padded.shape[2], 1), 0)
        row_pos = lax.broadcasted_iota(jnp.int32, (1, padded.shape[3]), 1)
        lower = 3 - 1
        west = column_strip[0][:, :, None, lower : lower + nest_rows + 2 * 1]
        east = column_strip[1][:, :, None, lower : lower + nest_rows + 2 * 1]
        south = row_strip[0][:, :, lower : lower + nest_cols + 2 * 1, None]
        north = row_strip[1][:, :, lower : lower + nest_cols + 2 * 1, None]
        result = jnp.where((index_x == 0) & (col_pos < 1), west, padded)
        result = jnp.where((index_x == count_x - 1) & (col_pos >= nest_cols + 1), east, result)
        result = jnp.where((index_y == 0) & (row_pos < 1), south, result)
        result = jnp.where((index_y == count_y - 1) & (row_pos >= nest_rows + 1), north, result)
        fields = advance(result)
    coarse = fields[:3].reshape(3, levels, coarse_cols, 3, coarse_rows, 3).mean(axis=(3, 5))
    col_first = index_x * parent_cols - shift_x
    rows_first = index_y * parent_rows - shift_y
    partial_block = place_along(
        lax.all_gather(coarse, "gy", axis=3, tiled=True), rows_first, parent_rows, 3
    )
    returned = place_along(
        lax.all_gather(partial_block, "gx", axis=2, tiled=True), col_first, parent_cols, 2
    )
    col_global = index_x * parent_cols + lax.broadcasted_iota(jnp.int32, (parent_cols, 1), 0)
    row_global = index_y * parent_rows + lax.broadcasted_iota(jnp.int32, (1, parent_rows), 1)
    inside = (
        (col_global >= shift_x)
        & (col_global < shift_x + span_x)
        & (row_global >= shift_y)
        & (row_global < shift_y + span_y)
    )
    blended = jnp.where(inside, returned, parent_next[:3])
    parent_out = jnp.concatenate([blended, parent_next[3:]], axis=0)
    return (fields, parent_out)


def solution(mesh):
    placed = (P(None, None, "gx", "gy"), P(None, None, "gx", "gy"), P(), P())
    return jax.shard_map(
        on_device,
        mesh=mesh,
        in_specs=placed,
        out_specs=(P(None, None, "gx", "gy"), P(None, None, "gx", "gy")),
        check_vma=False,
    )
```

profile of v0, /device:TPU:0, one launch (start us, length us, event | category | flops | bytes accessed | tf_op | source)
XLA Modules:
  0.0 323.4 jit_solution(11506212641012016978)
XLA Ops:
  8.0 2.2 fusion.95
  10.2 0.7 pad_maximum_fusion.29
  10.9 1.2 fusion.96
  12.1 2.4 collective-permute-start
  14.4 1.3 collective-permute-start.1
  16.5 0.3 constant_dynamic-slice_fusion.3
  17.0 0.3 copy.60
  17.4 39.1 %psum.14 = f32[2,4,8,24]{2,1,0,3:T(4,128)S(1)} all-reduce(f32[2,4,8,24]{2,1,0,3:T(4,128)S(1)} %copy.41), channel_id=1, replica_groups=mesh['gx'=4,'gy'=8] {'gy'}, use_global_device_ids=true, to_apply=%region_0.1 | all-reduce | flops 1536 | bytes 12288 | tf_op jit(solution)/shard_map/psum | solution.py:92
  56.5 9.2 %all_gather.12 = f32[2,4,8,96]{2,1,0,3:T(4,128)S(1)} all-gather(f32[2,4,8,24]{2,1,0,3:T(4,128)S(1)} %psum.14), channel_id=1, replica_groups=mesh['gx'=4,'gy'=8] {'gx'}, dimensions={3}, use_global_device_ids=true | all-gather | bytes 30720 | tf_op jit(solution)/shard_map/all_gather | solution.py:99
  65.7 0.5 fusion.33
  66.6 1.3 pad_maximum_fusion.28
  67.9 2.1 collective-permute-start.2
  70.0 1.3 collective-permute-start.3
  71.3 50.3 %all_gather.13 = f32[2,4,8,3072]{3,2,1,0:T(8,128)S(1)} all-gather(f32[2,4,8,384]{3,2,1,0:T(8,128)} %all-reduce.2.cloned.1.call-done), channel_id=1, replica_groups=mesh['gx'=4,'gy'=8] {'gy'}, dimensions={3}, use_global_device_ids=true | all-gather | bytes 884736 | tf_op jit(solution)/shard_map/all_gather | solution.py:96
  121.6 1.1 fusion.10
  123.1 0.3 copy.50
  123.4 0.3 copy.51
  123.9 0.3 copy.52
  124.2 3.1 fusion.2
  127.2 1.0 fusion.25
  128.3 0.3 slice_bitcast_fusion.5
  129.0 0.6 fusion.65
  129.6 1.3 collective-permute-start.4
  130.9 1.3 collective-permute-start.5
  132.2 1.3 collective-permute-start.12
  133.5 5.1 %collective-permute-start.13 = (f32[4,8,1,384]{3,2,1,0:T(1,128)}, f32[4,8,1,384]{3,2,1,0:T(1,128)S(1)}, u32[]{:S(2)}, u32[]{:S(2)}) collective-permute-start(f32[4,8,1,384]{3,2,1,0:T(1,128)} %get-tuple-element.58), channel_id=1, source_target_pairs={{0,8},{8,16},{16,24},{1,9},{9,17},{17,25},{2,10},{10,18},{18,26},{... | collective-permute-start | bytes 147464 | tf_op jit(solution)/shard_map/ppermute | solution.py:19
  138.7 0.3 pad_maximum_fusion.25
  138.9 1.3 collective-permute-start.6
  140.3 1.5 collective-permute-start.7
  141.8 0.8 fusion.94
  142.6 20.1 %collective-permute-done.6 = f32[4,8,26,1]{3,2,1,0:T(8,128)S(1)} collective-permute-done((f32[4,8,26,1]{3,2,1,0:T(8,128)S(1)}, f32[4,8,26,1]{3,2,1,0:T(8,128)S(1)}, u32[]{:S(2)}, u32[]{:S(2)}) %collective-permute-start.6) | collective-permute-done | bytes 3360 | tf_op jit(solution)/shard_map/ppermute | solution.py:19
  162.7 2.6 fusion.5
  165.4 1.0 fusion.23
  166.4 0.3 slice_bitcast_fusion.3
  167.1 0.6 fusion.57
  167.7 3.1 collective-permute-start.8
  170.8 1.3 collective-permute-start.9
  172.1 0.6 fusion.93
  172.7 1.5 collective-permute-done.9
  174.2 0.3 pad_maximum_fusion.19
  174.5 4.4 %collective-permute-start.10 = (f32[4,8,26,1]{3,2,1,0:T(8,128)S(1)}, f32[4,8,26,1]{3,2,1,0:T(8,128)S(1)}, u32[]{:S(2)}, u32[]{:S(2)}) collective-permute-start(f32[4,8,26,1]{3,2,1,0:T(8,128)S(1)} %get-tuple-element.46), channel_id=1, source_target_pairs={{0,1},{1,2},{2,3},{3,4},{4,5},{5,6},{6,7},{8,9},{9,10},{10,11},{11... | collective-permute-start | bytes 9992 | tf_op jit(solution)/shard_map/ppermute | solution.py:19
  178.9 1.3 collective-permute-start.11
  180.3 20.3 %collective-permute-done.10 = f32[4,8,26,1]{3,2,1,0:T(8,128)S(1)} collective-permute-done((f32[4,8,26,1]{3,2,1,0:T(8,128)S(1)}, f32[4,8,26,1]{3,2,1,0:T(8,128)S(1)}, u32[]{:S(2)}, u32[]{:S(2)}) %collective-permute-start.10) | collective-permute-done | bytes 3360 | tf_op jit(solution)/shard_map/ppermute | solution.py:19
  200.6 2.6 fusion.8
  203.2 1.0 fusion.21
  204.2 0.3 slice_bitcast_fusion.1
  204.9 1.2 fusion.49
  206.2 8.3 %copy.53 = f32[3,8,24,384]{1,3,2,0:T(8,128)} copy(f32[3,8,24,384]{3,2,1,0:T(8,128)S(1)} %pad_maximum_fusion.10) | data formatting | bytes 1769472 | tf_op jit(solution)/shard_map/stack | solution.py:41
  214.4 21.9 %reshape.170 = f32[3,8,8,3,128,3]{1,5,4,3,2,0:T(4,128)} reshape(f32[3,8,24,384]{1,3,2,0:T(8,128)} %copy.53) | data formatting | bytes 1769472 | tf_op jit(solution)/shard_map/reshape | solution.py:120
  236.3 14.8 %reduce_sum.9 = f32[3,8,8,128]{1,3,2,0:T(8,128)S(1)} reduce(f32[3,8,8,3,128,3]{1,5,4,3,2,0:T(4,128)} %reshape.170, f32[]{:T(128)} %constant.17.clone.1), dimensions={3,5}, to_apply=%region_2.3 | reduce | flops 196608 | bytes 983044 | tf_op jit(solution)/shard_map/reduce_sum | solution.py:120
  251.1 0.4 copy.54
  251.6 36.0 %all_gather.14 = f32[3,8,8,1024]{3,2,1,0:T(8,128)S(1)} all-gather(f32[3,8,8,128]{3,2,1,0:T(8,128)S(1)} %broadcast_multiply_fusion), channel_id=1, replica_groups=mesh['gx'=4,'gy'=8] {'gy'}, dimensions={3}, use_global_device_ids=true | all-gather | bytes 884736 | tf_op jit(solution)/shard_map/all_gather | solution.py:124
  287.6 1.7 fusion.13
  289.6 0.3 pad_maximum_fusion.13
  289.8 1.3 collective-permute-start.14
  291.1 4.6 %collective-permute-start.15 = (f32[4,8,26,1]{3,2,1,0:T(8,128)S(1)}, f32[4,8,26,1]{3,2,1,0:T(8,128)S(1)}, u32[]{:S(2)}, u32[]{:S(2)}) collective-permute-start(f32[4,8,26,1]{3,2,1,0:T(8,128)S(1)} %get-tuple-element.45), channel_id=1, source_target_pairs={{0,1},{1,2},{2,3},{3,4},{4,5},{5,6},{6,7},{8,9},{9,10},{10,11},{11... | collective-permute-start | bytes 9992 | tf_op jit(solution)/shard_map/ppermute | solution.py:19
  295.7 5.2 %collective-permute-done.14 = f32[4,8,26,1]{3,2,1,0:T(8,128)S(1)} collective-permute-done((f32[4,8,26,1]{3,2,1,0:T(8,128)S(1)}, f32[4,8,26,1]{3,2,1,0:T(8,128)S(1)}, u32[]{:S(2)}, u32[]{:S(2)}) %collective-permute-start.14) | collective-permute-done | bytes 3360 | tf_op jit(solution)/shard_map/ppermute | solution.py:20
  300.9 8.2 %collective-permute-done.15 = f32[4,8,26,1]{3,2,1,0:T(8,128)S(1)} collective-permute-done((f32[4,8,26,1]{3,2,1,0:T(8,128)S(1)}, f32[4,8,26,1]{3,2,1,0:T(8,128)S(1)}, u32[]{:S(2)}, u32[]{:S(2)}) %collective-permute-start.15) | collective-permute-done | bytes 3360 | tf_op jit(solution)/shard_map/ppermute | solution.py:19
  309.2 1.2 fusion.19
  310.6 0.8 copy-done.6
  311.5 1.0 fusion.41
  312.5 1.1 pad_maximum_fusion.8
  313.6 1.8 fusion.15
  315.5 1.1 pad_maximum_fusion.9
  (80 shorter events, 3.5 us)
Async XLA Ops:
  7.2 9.3 %copy-start = (f32[4,8,24,384]{3,2,1,0:T(8,128)S(1)}, f32[4,8,24,384]{3,2,1,0:T(8,128)}, u32[]{:S(2)}) copy-start(f32[4,8,24,384]{3,2,1,0:T(8,128)} %param.5) | copy-start | bytes 3538948
  7.2 64.1 %all-reduce.2.cloned.1.call-start = ((), (), s32[]{:S(2)}) async-start(), calls=%async_computation | async-start | bytes 196608 | tf_op jit(solution)/shard_map/psum | solution.py:85
  10.8 302.8 %all-gather.2.cloned.1.call-start = ((), (), s32[]{:S(2)}) async-start(), calls=%async_computation.1 | async-start | bytes 1474560 | tf_op jit(solution)/shard_map/all_gather | solution.py:127
  12.1 54.6 %collective-permute-start = (f32[4,8,1,384]{3,2,1,0:T(1,128)S(1)}, f32[4,8,1,384]{3,2,1,0:T(1,128)S(1)}, u32[]{:S(2)}, u32[]{:S(2)}) collective-permute-start(f32[4,8,1,384]{3,2,1,0:T(1,128)S(1)} %get-tuple-element.68), channel_id=1, source_target_pairs={{0,8},{8,16},{16,24},{1,9},{9,17},{17,25},{2,10},{10,18},{18,26},{... | collective-permute-start | bytes 147464 | tf_op jit(solution)/shard_map/ppermute | solution.py:19
  14.4 52.2 %collective-permute-start.1 = (f32[4,8,1,384]{3,2,1,0:T(1,128)S(1)}, f32[4,8,1,384]{3,2,1,0:T(1,128)S(1)}, u32[]{:S(2)}, u32[]{:S(2)}) collective-permute-start(f32[4,8,1,384]{3,2,1,0:T(1,128)S(1)} %get-tuple-element.69), channel_id=1, source_target_pairs={{8,0},{16,8},{24,16},{9,1},{17,9},{25,17},{10,2},{18,10},{26,18},{... | collective-permute-start | bytes 147464 | tf_op jit(solution)/shard_map/ppermute | solution.py:20
  17.0 49.7 %copy-start.1 = (f32[4,8,24,384]{3,2,1,0:T(8,128)S(1)}, f32[4,8,24,384]{3,2,1,0:T(8,128)}, u32[]{:S(2)}) copy-start(f32[4,8,24,384]{3,2,1,0:T(8,128)} %param.4) | copy-start | bytes 3538948
  67.9 56.3 %collective-permute-start.2 = (f32[4,8,26,1]{3,2,1,0:T(8,128)}, f32[4,8,26,1]{3,2,1,0:T(8,128)}, u32[]{:S(2)}, u32[]{:S(2)}) collective-permute-start(f32[4,8,26,1]{3,2,1,0:T(8,128)} %get-tuple-element.50), channel_id=1, source_target_pairs={{0,1},{1,2},{2,3},{3,4},{4,5},{5,6},{6,7},{8,9},{9,10},{10,11},{11... | collective-permute-start | bytes 9992 | tf_op jit(solution)/shard_map/ppermute | solution.py:19
  70.0 54.2 %collective-permute-start.3 = (f32[4,8,26,1]{3,2,1,0:T(8,128)}, f32[4,8,26,1]{3,2,1,0:T(8,128)}, u32[]{:S(2)}, u32[]{:S(2)}) collective-permute-start(f32[4,8,26,1]{3,2,1,0:T(8,128)} %get-tuple-element.51), channel_id=1, source_target_pairs={{1,0},{2,1},{3,2},{4,3},{5,4},{6,5},{7,6},{9,8},{10,9},{11,10},{12... | collective-permute-start | bytes 9992 | tf_op jit(solution)/shard_map/ppermute | solution.py:20
  129.6 9.0 %collective-permute-start.4 = (f32[4,8,1,384]{3,2,1,0:T(1,128)S(1)}, f32[4,8,1,384]{3,2,1,0:T(1,128)S(1)}, u32[]{:S(2)}, u32[]{:S(2)}) collective-permute-start(f32[4,8,1,384]{3,2,1,0:T(1,128)S(1)} %get-tuple-element.64), channel_id=1, source_target_pairs={{0,8},{8,16},{16,24},{1,9},{9,17},{17,25},{2,10},{10,18},{18,26},{... | collective-permute-start | bytes 147464 | tf_op jit(solution)/shard_map/ppermute | solution.py:19
  130.9 7.7 %collective-permute-start.5 = (f32[4,8,1,384]{3,2,1,0:T(1,128)S(1)}, f32[4,8,1,384]{3,2,1,0:T(1,128)S(1)}, u32[]{:S(2)}, u32[]{:S(2)}) collective-permute-start(f32[4,8,1,384]{3,2,1,0:T(1,128)S(1)} %get-tuple-element.65), channel_id=1, source_target_pairs={{8,0},{16,8},{24,16},{9,1},{17,9},{25,17},{10,2},{18,10},{26,18},{... | collective-permute-start | bytes 147464 | tf_op jit(solution)/shard_map/ppermute | solution.py:20
  132.2 157.3 %collective-permute-start.12 = (f32[4,8,1,384]{3,2,1,0:T(1,128)}, f32[4,8,1,384]{3,2,1,0:T(1,128)S(1)}, u32[]{:S(2)}, u32[]{:S(2)}) collective-permute-start(f32[4,8,1,384]{3,2,1,0:T(1,128)} %get-tuple-element.59), channel_id=1, source_target_pairs={{8,0},{16,8},{24,16},{9,1},{17,9},{25,17},{10,2},{18,10},{26,18},{... | collective-permute-start | bytes 147464 | tf_op jit(solution)/shard_map/ppermute | solution.py:20
  133.5 156.0 %collective-permute-start.13 = (f32[4,8,1,384]{3,2,1,0:T(1,128)}, f32[4,8,1,384]{3,2,1,0:T(1,128)S(1)}, u32[]{:S(2)}, u32[]{:S(2)}) collective-permute-start(f32[4,8,1,384]{3,2,1,0:T(1,128)} %get-tuple-element.58), channel_id=1, source_target_pairs={{0,8},{8,16},{16,24},{1,9},{9,17},{17,25},{2,10},{10,18},{18,26},{... | collective-permute-start | bytes 147464 | tf_op jit(solution)/shard_map/ppermute | solution.py:19
  138.9 23.8 %collective-permute-start.6 = (f32[4,8,26,1]{3,2,1,0:T(8,128)S(1)}, f32[4,8,26,1]{3,2,1,0:T(8,128)S(1)}, u32[]{:S(2)}, u32[]{:S(2)}) collective-permute-start(f32[4,8,26,1]{3,2,1,0:T(8,128)S(1)} %get-tuple-element.48), channel_id=1, source_target_pairs={{0,1},{1,2},{2,3},{3,4},{4,5},{5,6},{6,7},{8,9},{9,10},{10,11},{11... | collective-permute-start | bytes 9992 | tf_op jit(solution)/shard_map/ppermute | solution.py:19
  140.3 22.5 %collective-permute-start.7 = (f32[4,8,26,1]{3,2,1,0:T(8,128)S(1)}, f32[4,8,26,1]{3,2,1,0:T(8,128)S(1)}, u32[]{:S(2)}, u32[]{:S(2)}) collective-permute-start(f32[4,8,26,1]{3,2,1,0:T(8,128)S(1)} %get-tuple-element.49), channel_id=1, source_target_pairs={{1,0},{2,1},{3,2},{4,3},{5,4},{6,5},{7,6},{9,8},{10,9},{11,10},{12... | collective-permute-start | bytes 9992 | tf_op jit(solution)/shard_map/ppermute | solution.py:20
  167.7 5.0 %collective-permute-start.8 = (f32[4,8,1,384]{3,2,1,0:T(1,128)S(1)}, f32[4,8,1,384]{3,2,1,0:T(1,128)S(1)}, u32[]{:S(2)}, u32[]{:S(2)}) collective-permute-start(f32[4,8,1,384]{3,2,1,0:T(1,128)S(1)} %get-tuple-element.62), channel_id=1, source_target_pairs={{0,8},{8,16},{16,24},{1,9},{9,17},{17,25},{2,10},{10,18},{18,26},{... | collective-permute-start | bytes 147464 | tf_op jit(solution)/shard_map/ppermute | solution.py:19
  170.8 3.4 %collective-permute-start.9 = (f32[4,8,1,384]{3,2,1,0:T(1,128)S(1)}, f32[4,8,1,384]{3,2,1,0:T(1,128)S(1)}, u32[]{:S(2)}, u32[]{:S(2)}) collective-permute-start(f32[4,8,1,384]{3,2,1,0:T(1,128)S(1)} %get-tuple-element.63), channel_id=1, source_target_pairs={{8,0},{16,8},{24,16},{9,1},{17,9},{25,17},{10,2},{18,10},{26,18},{... | collective-permute-start | bytes 147464 | tf_op jit(solution)/shard_map/ppermute | solution.py:20
  174.5 26.0 %collective-permute-start.10 = (f32[4,8,26,1]{3,2,1,0:T(8,128)S(1)}, f32[4,8,26,1]{3,2,1,0:T(8,128)S(1)}, u32[]{:S(2)}, u32[]{:S(2)}) collective-permute-start(f32[4,8,26,1]{3,2,1,0:T(8,128)S(1)} %get-tuple-element.46), channel_id=1, source_target_pairs={{0,1},{1,2},{2,3},{3,4},{4,5},{5,6},{6,7},{8,9},{9,10},{10,11},{11... | collective-permute-start | bytes 9992 | tf_op jit(solution)/shard_map/ppermute | solution.py:19
  178.9 21.6 %collective-permute-start.11 = (f32[4,8,26,1]{3,2,1,0:T(8,128)S(1)}, f32[4,8,26,1]{3,2,1,0:T(8,128)S(1)}, u32[]{:S(2)}, u32[]{:S(2)}) collective-permute-start(f32[4,8,26,1]{3,2,1,0:T(8,128)S(1)} %get-tuple-element.47), channel_id=1, source_target_pairs={{1,0},{2,1},{3,2},{4,3},{5,4},{6,5},{7,6},{9,8},{10,9},{11,10},{12... | collective-permute-start | bytes 9992 | tf_op jit(solution)/shard_map/ppermute | solution.py:20
  206.1 8.3 %copy-start.2 = (f32[1,8,24,384]{3,2,1,0:T(8,128)}, f32[1,8,24,384]{3,2,1,0:T(8,128)S(1)}, u32[]{:S(2)}) copy-start(f32[1,8,24,384]{3,2,1,0:T(8,128)S(1)} %get-tuple-element.11) | copy-start | bytes 884740
  289.8 11.1 %collective-permute-start.14 = (f32[4,8,26,1]{3,2,1,0:T(8,128)S(1)}, f32[4,8,26,1]{3,2,1,0:T(8,128)S(1)}, u32[]{:S(2)}, u32[]{:S(2)}) collective-permute-start(f32[4,8,26,1]{3,2,1,0:T(8,128)S(1)} %get-tuple-element.44), channel_id=1, source_target_pairs={{1,0},{2,1},{3,2},{4,3},{5,4},{6,5},{7,6},{9,8},{10,9},{11,10},{12... | collective-permute-start | bytes 9992 | tf_op jit(solution)/shard_map/ppermute | solution.py:20
  291.1 18.0 %collective-permute-start.15 = (f32[4,8,26,1]{3,2,1,0:T(8,128)S(1)}, f32[4,8,26,1]{3,2,1,0:T(8,128)S(1)}, u32[]{:S(2)}, u32[]{:S(2)}) collective-permute-start(f32[4,8,26,1]{3,2,1,0:T(8,128)S(1)} %get-tuple-element.45), channel_id=1, source_target_pairs={{0,1},{1,2},{2,3},{3,4},{4,5},{5,6},{6,7},{8,9},{9,10},{10,11},{11... | collective-permute-start | bytes 9992 | tf_op jit(solution)/shard_map/ppermute | solution.py:19
  310.4 0.9 copy-start.6
  310.4 1.1 copy-start.7
  310.4 1.1 copy-start.8
  310.4 1.1 copy-start.9
  311.5 1.0 copy-start.3
  311.5 1.0 copy-start.4
  312.5 1.1 copy-start.5
Sparse Core Ops, SparseCore 0:
  11.0 34.0 all-reduce.1
  289.5 15.4 all-gather.1
where the time goes:
time: 325 us; the launch traced here: 323 us
  blocking collectives  135 us (42%)
  waiting for transfers between devices  55.4 us (17%)
  local copies, waits for them, and re-layouts  40.7 us (13%)
  other arithmetic  36.6 us (11%)
  starting transfers between devices  34.8 us (11%)
  between operations  16.1 us (5%)
  matrix products  5.11 us (2%)
    all_gather x1, blocking collectives, on_device(): lax.all_gather(columns, 'gy', axis=3, tiled=True)  50.3 us
    ppermute x8, waiting for transfers between devices, extended(): before = lax.ppermute(last, axis, up)  48.7 us
    psum x1, blocking collectives, on_device(): row_pair = lax.psum(row_pair, 'gy')  39.1 us
    all_gather x1, blocking collectives, on_device(): lax.all_gather(coarse, 'gy', axis=3, tiled=True)  36 us
    ppermute x8, starting transfers between devices, extended(): before = lax.ppermute(last, axis, up)  24.2 us
    reshape x1, local copies, waits for them, and re-layouts, on_device(): fields[:3].reshape(3, levels, coarse_cols, 3, coarse_rows, 3)  21.9 us
    reduce_sum x1, other arithmetic, on_device(): fields[:3].reshape(3, levels, coarse_cols, 3, coarse_rows, 3)  14.8 us
    ppermute x8, starting transfers between devices, extended(): after = lax.ppermute(initial, axis, down)  10.5 us
  transfers between devices with their start and end apart: 18, of which 5 were waited for; matrix products, arithmetic and copies ran while one was open for 22% of the time, Pallas kernels for 0%

commit v1 on v0

--- a/solution.py
+++ b/solution.py
@@ -7,6 +7,28 @@
 CARRY_RATE = 0.35
 SOUND_RATE = 0.4
 MIXING_RATE = 0.2
+
+
+def joined_along(pieces, dim):
+    shape = list(pieces.shape[1:])
+    shape[dim] *= pieces.shape[0]
+    return jnp.moveaxis(pieces, 0, dim).reshape(shape)
+
+
+def doubled(x, axis):
+    size = lax.axis_size(axis)
+    blocks = x[None]
+    for level in range(size.bit_length() - 1):
+        bit = 1 << level
+        other = lax.ppermute(blocks, axis, [(i, i ^ bit) for i in range(size)])
+        both = jnp.stack([blocks, other])
+        upper = lax.axis_index(axis) >> level & 1
+        blocks = jnp.where(upper == 0, both, both[::-1]).reshape(-1, *x.shape)
+    return blocks
+
+
+def doubled_up(value, axis, dim):
+    return joined_along(doubled(value, axis), dim)
 
 
 def extended(value, sides, width):
@@ -120,9 +142,7 @@
     coarse = fields[:3].reshape(3, levels, coarse_cols, 3, coarse_rows, 3).mean(axis=(3, 5))
     col_first = index_x * parent_cols - shift_x
     rows_first = index_y * parent_rows - shift_y
-    partial_block = place_along(
-        lax.all_gather(coarse, "gy", axis=3, tiled=True), rows_first, parent_rows, 3
-    )
+    partial_block = place_along(doubled_up(coarse, "gy", 3), rows_first, parent_rows, 3)
     returned = place_along(
         lax.all_gather(partial_block, "gx", axis=2, tiled=True), col_first, parent_cols, 2
     )

time: 325 us -> 342 us (1.052)
  blocking collectives: 135 us -> 98.6 us
  waiting for transfers between devices: 55.4 us -> 86 us
  starting transfers between devices: 34.8 us -> 43.2 us
  local copies, waits for them, and re-layouts: 40.7 us -> 48 us
  other arithmetic: 36.6 us -> 43.3 us
    all_gather x1 -> x0, blocking collectives: 36 us -> none  [on_device(): lax.all_gather(coarse, 'gy', axis=3, tiled=True)]
    ppermute x0 -> x3, waiting for transfers between devices: none -> 20.2 us  [doubled(): other = lax.ppermute(blocks, axis, [(i, i ^ bit) for i in range(size)])]
    ppermute x0 -> x3, starting transfers between devices: none -> 9.62 us  [doubled(): other = lax.ppermute(blocks, axis, [(i, i ^ bit) for i in range(size)])]
    ppermute x8, waiting for transfers between devices: 6.69 us -> 14.9 us  [extended(): after = lax.ppermute(initial, axis, down)]
    another operation x0 -> x4, other arithmetic: none -> 5.33 us  [doubled(): both = jnp.stack([blocks, other])]
  transfers between devices with their start and end apart: 18 -> 21, of which waited for: 5 -> 8; matrix products, arithmetic and copies ran while one was open for 22% -> 5% of each run, Pallas kernels for 0% -> 0%
where the time goes in v1:
time: 342 us; the launch traced here: 340 us
  blocking collectives  98.6 us (29%)
  waiting for transfers between devices  86 us (25%)
  local copies, waits for them, and re-layouts  48 us (14%)
  other arithmetic  43.3 us (13%)
  starting transfers between devices  43.2 us (13%)
  between operations  16.1 us (5%)
  matrix products  5.09 us (1%)
    ppermute x8, waiting for transfers between devices, extended(): before = lax.ppermute(last, axis, up)  50.8 us
    all_gather x1, blocking collectives, on_device(): lax.all_gather(columns, 'gy', axis=3, tiled=True)  50.3 us
    psum x1, blocking collectives, on_device(): row_pair = lax.psum(row_pair, 'gy')  39.1 us
    ppermute x8, starting transfers between devices, extended(): before = lax.ppermute(last, axis, up)  23 us
    reshape x1, local copies, waits for them, and re-layouts, on_device(): fields[:3].reshape(3, levels, coarse_cols, 3, coarse_rows, 3)  21.9 us
    ppermute x3, waiting for transfers between devices, doubled(): other = lax.ppermute(blocks, axis, [(i, i ^ bit) for i in range(size)])  20.2 us
    ppermute x8, waiting for transfers between devices, extended(): after = lax.ppermute(initial, axis, down)  14.9 us
    reduce_sum x1, other arithmetic, on_device(): fields[:3].reshape(3, levels, coarse_cols, 3, coarse_rows, 3)  14.8 us
  transfers between devices with their start and end apart: 21, of which 8 were waited for; matrix products, arithmetic and copies ran while one was open for 5% of the time, Pallas kernels for 0%

profile of v1, /device:TPU:0, one launch (start us, length us, event | category | flops | bytes accessed | tf_op | source)
XLA Modules:
  0.0 340.3 jit_solution(8165883914323433441)
XLA Ops:
  8.0 2.2 fusion.97
  10.1 0.6 pad_maximum_fusion.32
  10.9 1.2 fusion.98
  12.0 2.4 collective-permute-start
  14.4 1.3 collective-permute-start.1
  17.4 39.1 %psum.14 = f32[2,4,8,24]{2,1,0,3:T(4,128)S(1)} all-reduce(f32[2,4,8,24]{2,1,0,3:T(4,128)S(1)} %copy.64), channel_id=1, replica_groups=mesh['gx'=4,'gy'=8] {'gy'}, use_global_device_ids=true, to_apply=%region_0.1 | all-reduce | flops 1536 | bytes 12288 | tf_op jit(solution)/shard_map/psum | solution.py:114
  56.5 9.2 %all_gather.9 = f32[2,4,8,96]{2,1,0,3:T(4,128)S(1)} all-gather(f32[2,4,8,24]{2,1,0,3:T(4,128)S(1)} %psum.14), channel_id=1, replica_groups=mesh['gx'=4,'gy'=8] {'gx'}, dimensions={3}, use_global_device_ids=true | all-gather | bytes 30720 | tf_op jit(solution)/shard_map/all_gather | solution.py:121
  65.6 0.5 fusion.35
  66.6 1.3 pad_maximum_fusion.30
  67.9 2.1 collective-permute-start.2
  70.0 1.3 collective-permute-start.3
  71.3 50.3 %all_gather.10 = f32[2,4,8,3072]{3,2,1,0:T(8,128)S(1)} all-gather(f32[2,4,8,384]{3,2,1,0:T(8,128)} %all-reduce.2.cloned.1.call-done), channel_id=1, replica_groups=mesh['gx'=4,'gy'=8] {'gy'}, dimensions={3}, use_global_device_ids=true | all-gather | bytes 884736 | tf_op jit(solution)/shard_map/all_gather | solution.py:118
  121.6 1.1 fusion.12
  124.1 3.1 fusion.4
  127.2 1.0 fusion.27
  129.0 0.6 fusion.67
  129.6 1.3 collective-permute-start.4
  130.9 1.3 collective-permute-start.5
  132.2 3.2 collective-permute-done.5
  135.8 1.3 collective-permute-start.6
  137.1 1.5 collective-permute-start.7
  138.6 19.9 %collective-permute-done.6 = f32[4,8,26,1]{3,2,1,0:T(8,128)S(1)} collective-permute-done((f32[4,8,26,1]{3,2,1,0:T(8,128)S(1)}, f32[4,8,26,1]{3,2,1,0:T(8,128)S(1)}, u32[]{:S(2)}, u32[]{:S(2)}) %collective-permute-start.6) | collective-permute-done | bytes 3360 | tf_op jit(solution)/shard_map/ppermute | solution.py:41
  158.4 2.6 fusion.7
  161.1 1.0 fusion.25
  162.8 0.6 fusion.59
  163.5 4.2 %collective-permute-start.8 = (f32[4,8,1,384]{3,2,1,0:T(1,128)S(1)}, f32[4,8,1,384]{3,2,1,0:T(1,128)S(1)}, u32[]{:S(2)}, u32[]{:S(2)}) collective-permute-start(f32[4,8,1,384]{3,2,1,0:T(1,128)S(1)} %get-tuple-element.66), channel_id=1, source_target_pairs={{0,8},{8,16},{16,24},{1,9},{9,17},{17,25},{2,10},{10,18},{18,26},{... | collective-permute-start | bytes 147464 | tf_op jit(solution)/shard_map/ppermute | solution.py:41
  167.7 1.3 collective-permute-start.9
  169.0 1.8 collective-permute-done.9
  171.1 4.1 %collective-permute-start.10 = (f32[4,8,26,1]{3,2,1,0:T(8,128)S(1)}, f32[4,8,26,1]{3,2,1,0:T(8,128)S(1)}, u32[]{:S(2)}, u32[]{:S(2)}) collective-permute-start(f32[4,8,26,1]{3,2,1,0:T(8,128)S(1)} %get-tuple-element.50), channel_id=1, source_target_pairs={{0,1},{1,2},{2,3},{3,4},{4,5},{5,6},{6,7},{8,9},{9,10},{10,11},{11... | collective-permute-start | bytes 9992 | tf_op jit(solution)/shard_map/ppermute | solution.py:41
  175.2 1.3 collective-permute-start.11
  176.5 20.7 %collective-permute-done.10 = f32[4,8,26,1]{3,2,1,0:T(8,128)S(1)} collective-permute-done((f32[4,8,26,1]{3,2,1,0:T(8,128)S(1)}, f32[4,8,26,1]{3,2,1,0:T(8,128)S(1)}, u32[]{:S(2)}, u32[]{:S(2)}) %collective-permute-start.10) | collective-permute-done | bytes 3360 | tf_op jit(solution)/shard_map/ppermute | solution.py:41
  197.2 2.6 fusion.10
  199.8 1.0 fusion.23
  201.5 1.2 fusion.51
  202.8 8.3 %copy.76 = f32[3,8,24,384]{1,3,2,0:T(8,128)} copy(f32[3,8,24,384]{3,2,1,0:T(8,128)S(1)} %pad_maximum_fusion.11) | data formatting | bytes 1769472 | tf_op jit(solution)/shard_map/stack | solution.py:63
  211.1 21.9 %reshape.200 = f32[3,8,8,3,128,3]{1,5,4,3,2,0:T(4,128)} reshape(f32[3,8,24,384]{1,3,2,0:T(8,128)} %copy.76) | data formatting | bytes 1769472 | tf_op jit(solution)/shard_map/reshape | solution.py:142
  232.9 14.8 %reduce_sum.9 = f32[3,8,8,128]{1,3,2,0:T(8,128)S(1)} reduce(f32[3,8,8,3,128,3]{1,5,4,3,2,0:T(4,128)} %reshape.200, f32[]{:T(128)} %constant.17.clone.1), dimensions={3,5}, to_apply=%region_2.3 | reduce | flops 196608 | bytes 983044 | tf_op jit(solution)/shard_map/reduce_sum | solution.py:142
  247.7 2.0 multiply_bitcast_fusion.1
  249.7 1.8 copy.77
  251.6 2.5 collective-permute-start.12
  254.1 3.0 collective-permute-done.12
  257.1 0.5 copy.78
  257.6 1.7 pad_maximum_fusion
  259.3 3.5 %fusion.1 = (f32[1,2,3,8,8,128]{3,5,4,2,1,0:T(8,128)}, f32[2,3,8,8,128]{2,4,3,1,0:T(8,128)}) fusion(f32[2,1,3,8,8,128]{3,5,4,2,1,0:T(8,128)S(1)} %pad_maximum_fusion, pred[]{:T(512)S(6)} %eq.49), kind=kLoop, calls=%fused_computation.3 | loop fusion | flops 49152 | bytes 589825 | tf_op jit(solution)/shard_map/stack;reshape | solution.py:24
  262.8 2.3 copy.79
  265.2 4.7 %collective-permute-start.13 = (f32[2,3,8,8,128]{4,3,2,1,0:T(8,128)S(1)}, f32[2,3,8,8,128]{4,3,2,1,0:T(8,128)S(1)}, u32[]{:S(2)}, u32[]{:S(2)}) collective-permute-start(f32[2,3,8,8,128]{4,3,2,1,0:T(8,128)S(1)} %copy.79), channel_id=1, source_target_pairs={{0,2},{1,3},{2,0},{3,1},{4,6},{5,7},{6,4},{7,5},{8,10},{9,11},{10,... | collective-permute-start | bytes 589832 | tf_op jit(solution)/shard_map/ppermute | solution.py:23
  269.8 1.3 collective-permute-start.15
  271.1 3.0 collective-permute-start.16
  274.2 2.3 copy.80
  276.6 2.4 collective-permute-start.14
  279.0 0.8 fusion.96
  279.8 17.1 %collective-permute-done.14 = f32[4,3,8,8,128]{4,3,2,1,0:T(8,128)S(1)} collective-permute-done((f32[4,3,8,8,128]{4,3,2,1,0:T(8,128)S(1)}, f32[4,3,8,8,128]{4,3,2,1,0:T(8,128)S(1)}, u32[]{:S(2)}, u32[]{:S(2)}) %collective-permute-start.14) | collective-permute-done | bytes 393248 | tf_op jit(solution)/shard_map/ppermute | solution.py:23
  297.1 0.5 copy.99
  297.7 1.7 fusion.15
  299.9 1.3 collective-permute-start.17
  301.2 4.6 %collective-permute-start.18 = (f32[4,8,26,1]{3,2,1,0:T(8,128)S(1)}, f32[4,8,26,1]{3,2,1,0:T(8,128)S(1)}, u32[]{:S(2)}, u32[]{:S(2)}) collective-permute-start(f32[4,8,26,1]{3,2,1,0:T(8,128)S(1)} %get-tuple-element.49), channel_id=1, source_target_pairs={{0,1},{1,2},{2,3},{3,4},{4,5},{5,6},{6,7},{8,9},{9,10},{10,11},{11... | collective-permute-start | bytes 9992 | tf_op jit(solution)/shard_map/ppermute | solution.py:41
  305.8 9.9 %collective-permute-done.17 = f32[4,8,26,1]{3,2,1,0:T(8,128)S(1)} collective-permute-done((f32[4,8,26,1]{3,2,1,0:T(8,128)S(1)}, f32[4,8,26,1]{3,2,1,0:T(8,128)S(1)}, u32[]{:S(2)}, u32[]{:S(2)}) %collective-permute-start.17) | collective-permute-done | bytes 3360 | tf_op jit(solution)/shard_map/ppermute | solution.py:42
  315.7 10.3 %collective-permute-done.18 = f32[4,8,26,1]{3,2,1,0:T(8,128)S(1)} collective-permute-done((f32[4,8,26,1]{3,2,1,0:T(8,128)S(1)}, f32[4,8,26,1]{3,2,1,0:T(8,128)S(1)}, u32[]{:S(2)}, u32[]{:S(2)}) %collective-permute-start.18) | collective-permute-done | bytes 3360 | tf_op jit(solution)/shard_map/ppermute | solution.py:41
  326.0 1.2 fusion.21
  327.4 0.8 copy-done.5
  328.6 0.7 copy-done.3
  329.4 1.1 pad_maximum_fusion.9
  330.5 1.8 fusion.17
  332.3 1.1 pad_maximum_fusion.10
  (90 shorter events, 7.2 us)
Async XLA Ops:
  7.2 9.2 %copy-start = (f32[4,8,24,384]{3,2,1,0:T(8,128)S(1)}, f32[4,8,24,384]{3,2,1,0:T(8,128)}, u32[]{:S(2)}) copy-start(f32[4,8,24,384]{3,2,1,0:T(8,128)} %param.5) | copy-start | bytes 3538948
  7.2 64.1 %all-reduce.2.cloned.1.call-start = ((), (), s32[]{:S(2)}) async-start(), calls=%async_computation | async-start | bytes 196608 | tf_op jit(solution)/shard_map/psum | solution.py:107
  10.8 319.7 %all-gather.2.cloned.1.call-start = ((), (), s32[]{:S(2)}) async-start(), calls=%async_computation.1 | async-start | bytes 1474560 | tf_op jit(solution)/shard_map/all_gather | solution.py:147
  12.0 54.6 %collective-permute-start = (f32[4,8,1,384]{3,2,1,0:T(1,128)S(1)}, f32[4,8,1,384]{3,2,1,0:T(1,128)S(1)}, u32[]{:S(2)}, u32[]{:S(2)}) collective-permute-start(f32[4,8,1,384]{3,2,1,0:T(1,128)S(1)} %get-tuple-element.72), channel_id=1, source_target_pairs={{0,8},{8,16},{16,24},{1,9},{9,17},{17,25},{2,10},{10,18},{18,26},{... | collective-permute-start | bytes 147464 | tf_op jit(solution)/shard_map/ppermute | solution.py:41
  14.4 52.2 %collective-permute-start.1 = (f32[4,8,1,384]{3,2,1,0:T(1,128)S(1)}, f32[4,8,1,384]{3,2,1,0:T(1,128)S(1)}, u32[]{:S(2)}, u32[]{:S(2)}) collective-permute-start(f32[4,8,1,384]{3,2,1,0:T(1,128)S(1)} %get-tuple-element.73), channel_id=1, source_target_pairs={{8,0},{16,8},{24,16},{9,1},{17,9},{25,17},{10,2},{18,10},{26,18},{... | collective-permute-start | bytes 147464 | tf_op jit(solution)/shard_map/ppermute | solution.py:42
  16.7 49.9 %copy-start.1 = (f32[4,8,24,384]{3,2,1,0:T(8,128)S(1)}, f32[4,8,24,384]{3,2,1,0:T(8,128)}, u32[]{:S(2)}) copy-start(f32[4,8,24,384]{3,2,1,0:T(8,128)} %param.4) | copy-start | bytes 3538948
  67.9 56.3 %collective-permute-start.2 = (f32[4,8,26,1]{3,2,1,0:T(8,128)}, f32[4,8,26,1]{3,2,1,0:T(8,128)}, u32[]{:S(2)}, u32[]{:S(2)}) collective-permute-start(f32[4,8,26,1]{3,2,1,0:T(8,128)} %get-tuple-element.54), channel_id=1, source_target_pairs={{0,1},{1,2},{2,3},{3,4},{4,5},{5,6},{6,7},{8,9},{9,10},{10,11},{11... | collective-permute-start | bytes 9992 | tf_op jit(solution)/shard_map/ppermute | solution.py:41
  70.0 54.2 %collective-permute-start.3 = (f32[4,8,26,1]{3,2,1,0:T(8,128)}, f32[4,8,26,1]{3,2,1,0:T(8,128)}, u32[]{:S(2)}, u32[]{:S(2)}) collective-permute-start(f32[4,8,26,1]{3,2,1,0:T(8,128)} %get-tuple-element.55), channel_id=1, source_target_pairs={{1,0},{2,1},{3,2},{4,3},{5,4},{6,5},{7,6},{9,8},{10,9},{11,10},{12... | collective-permute-start | bytes 9992 | tf_op jit(solution)/shard_map/ppermute | solution.py:42
  129.6 2.6 collective-permute-start.4
  130.9 4.5 %collective-permute-start.5 = (f32[4,8,1,384]{3,2,1,0:T(1,128)S(1)}, f32[4,8,1,384]{3,2,1,0:T(1,128)S(1)}, u32[]{:S(2)}, u32[]{:S(2)}) collective-permute-start(f32[4,8,1,384]{3,2,1,0:T(1,128)S(1)} %get-tuple-element.69), channel_id=1, source_target_pairs={{8,0},{16,8},{24,16},{9,1},{17,9},{25,17},{10,2},{18,10},{26,18},{... | collective-permute-start | bytes 147464 | tf_op jit(solution)/shard_map/ppermute | solution.py:42
  135.8 22.7 %collective-permute-start.6 = (f32[4,8,26,1]{3,2,1,0:T(8,128)S(1)}, f32[4,8,26,1]{3,2,1,0:T(8,128)S(1)}, u32[]{:S(2)}, u32[]{:S(2)}) collective-permute-start(f32[4,8,26,1]{3,2,1,0:T(8,128)S(1)} %get-tuple-element.52), channel_id=1, source_target_pairs={{0,1},{1,2},{2,3},{3,4},{4,5},{5,6},{6,7},{8,9},{9,10},{10,11},{11... | collective-permute-start | bytes 9992 | tf_op jit(solution)/shard_map/ppermute | solution.py:41
  137.1 21.3 %collective-permute-start.7 = (f32[4,8,26,1]{3,2,1,0:T(8,128)S(1)}, f32[4,8,26,1]{3,2,1,0:T(8,128)S(1)}, u32[]{:S(2)}, u32[]{:S(2)}) collective-permute-start(f32[4,8,26,1]{3,2,1,0:T(8,128)S(1)} %get-tuple-element.53), channel_id=1, source_target_pairs={{1,0},{2,1},{3,2},{4,3},{5,4},{6,5},{7,6},{9,8},{10,9},{11,10},{12... | collective-permute-start | bytes 9992 | tf_op jit(solution)/shard_map/ppermute | solution.py:42
  163.5 5.5 %collective-permute-start.8 = (f32[4,8,1,384]{3,2,1,0:T(1,128)S(1)}, f32[4,8,1,384]{3,2,1,0:T(1,128)S(1)}, u32[]{:S(2)}, u32[]{:S(2)}) collective-permute-start(f32[4,8,1,384]{3,2,1,0:T(1,128)S(1)} %get-tuple-element.66), channel_id=1, source_target_pairs={{0,8},{8,16},{16,24},{1,9},{9,17},{17,25},{2,10},{10,18},{18,26},{... | collective-permute-start | bytes 147464 | tf_op jit(solution)/shard_map/ppermute | solution.py:41
  167.7 3.1 collective-permute-start.9
  171.1 26.1 %collective-permute-start.10 = (f32[4,8,26,1]{3,2,1,0:T(8,128)S(1)}, f32[4,8,26,1]{3,2,1,0:T(8,128)S(1)}, u32[]{:S(2)}, u32[]{:S(2)}) collective-permute-start(f32[4,8,26,1]{3,2,1,0:T(8,128)S(1)} %get-tuple-element.50), channel_id=1, source_target_pairs={{0,1},{1,2},{2,3},{3,4},{4,5},{5,6},{6,7},{8,9},{9,10},{10,11},{11... | collective-permute-start | bytes 9992 | tf_op jit(solution)/shard_map/ppermute | solution.py:41
  175.2 22.0 %collective-permute-start.11 = (f32[4,8,26,1]{3,2,1,0:T(8,128)S(1)}, f32[4,8,26,1]{3,2,1,0:T(8,128)S(1)}, u32[]{:S(2)}, u32[]{:S(2)}) collective-permute-start(f32[4,8,26,1]{3,2,1,0:T(8,128)S(1)} %get-tuple-element.51), channel_id=1, source_target_pairs={{1,0},{2,1},{3,2},{4,3},{5,4},{6,5},{7,6},{9,8},{10,9},{11,10},{12... | collective-permute-start | bytes 9992 | tf_op jit(solution)/shard_map/ppermute | solution.py:42
  202.7 8.3 %copy-start.2 = (f32[1,8,24,384]{3,2,1,0:T(8,128)}, f32[1,8,24,384]{3,2,1,0:T(8,128)S(1)}, u32[]{:S(2)}) copy-start(f32[1,8,24,384]{3,2,1,0:T(8,128)S(1)} %get-tuple-element.13) | copy-start | bytes 884740
  251.6 5.5 %collective-permute-start.12 = (f32[1,3,8,8,128]{4,3,2,1,0:T(8,128)S(1)}, f32[1,3,8,8,128]{4,3,2,1,0:T(8,128)S(1)}, u32[]{:S(2)}, u32[]{:S(2)}) collective-permute-start(f32[1,3,8,8,128]{4,3,2,1,0:T(8,128)S(1)} %copy.77), channel_id=1, source_target_pairs={{0,1},{1,0},{2,3},{3,2},{4,5},{5,4},{6,7},{7,6},{8,9},{9,8},{10,11... | collective-permute-start | bytes 294920 | tf_op jit(solution)/shard_map/ppermute | solution.py:23
  265.2 11.3 %collective-permute-start.13 = (f32[2,3,8,8,128]{4,3,2,1,0:T(8,128)S(1)}, f32[2,3,8,8,128]{4,3,2,1,0:T(8,128)S(1)}, u32[]{:S(2)}, u32[]{:S(2)}) collective-permute-start(f32[2,3,8,8,128]{4,3,2,1,0:T(8,128)S(1)} %copy.79), channel_id=1, source_target_pairs={{0,2},{1,3},{2,0},{3,1},{4,6},{5,7},{6,4},{7,5},{8,10},{9,11},{10,... | collective-permute-start | bytes 589832 | tf_op jit(solution)/shard_map/ppermute | solution.py:23
  269.8 29.8 %collective-permute-start.15 = (f32[4,8,1,384]{3,2,1,0:T(1,128)}, f32[4,8,1,384]{3,2,1,0:T(1,128)S(1)}, u32[]{:S(2)}, u32[]{:S(2)}) collective-permute-start(f32[4,8,1,384]{3,2,1,0:T(1,128)} %get-tuple-element.63), channel_id=1, source_target_pairs={{8,0},{16,8},{24,16},{9,1},{17,9},{25,17},{10,2},{18,10},{26,18},{... | collective-permute-start | bytes 147464 | tf_op jit(solution)/shard_map/ppermute | solution.py:42
  271.1 28.5 %collective-permute-start.16 = (f32[4,8,1,384]{3,2,1,0:T(1,128)}, f32[4,8,1,384]{3,2,1,0:T(1,128)S(1)}, u32[]{:S(2)}, u32[]{:S(2)}) collective-permute-start(f32[4,8,1,384]{3,2,1,0:T(1,128)} %get-tuple-element.62), channel_id=1, source_target_pairs={{0,8},{8,16},{16,24},{1,9},{9,17},{17,25},{2,10},{10,18},{18,26},{... | collective-permute-start | bytes 147464 | tf_op jit(solution)/shard_map/ppermute | solution.py:41
  276.6 20.4 %collective-permute-start.14 = (f32[4,3,8,8,128]{4,3,2,1,0:T(8,128)S(1)}, f32[4,3,8,8,128]{4,3,2,1,0:T(8,128)S(1)}, u32[]{:S(2)}, u32[]{:S(2)}) collective-permute-start(f32[4,3,8,8,128]{4,3,2,1,0:T(8,128)S(1)} %bitcast.105), channel_id=1, source_target_pairs={{0,4},{1,5},{2,6},{3,7},{4,0},{5,1},{6,2},{7,3},{8,12},{9,13},{10,... | collective-permute-start | bytes 1179656 | tf_op jit(solution)/shard_map/ppermute | solution.py:23
  299.9 15.8 %collective-permute-start.17 = (f32[4,8,26,1]{3,2,1,0:T(8,128)S(1)}, f32[4,8,26,1]{3,2,1,0:T(8,128)S(1)}, u32[]{:S(2)}, u32[]{:S(2)}) collective-permute-start(f32[4,8,26,1]{3,2,1,0:T(8,128)S(1)} %get-tuple-element.48), channel_id=1, source_target_pairs={{1,0},{2,1},{3,2},{4,3},{5,4},{6,5},{7,6},{9,8},{10,9},{11,10},{12... | collective-permute-start | bytes 9992 | tf_op jit(solution)/shard_map/ppermute | solution.py:42
  301.2 24.8 %collective-permute-start.18 = (f32[4,8,26,1]{3,2,1,0:T(8,128)S(1)}, f32[4,8,26,1]{3,2,1,0:T(8,128)S(1)}, u32[]{:S(2)}, u32[]{:S(2)}) collective-permute-start(f32[4,8,26,1]{3,2,1,0:T(8,128)S(1)} %get-tuple-element.49), channel_id=1, source_target_pairs={{0,1},{1,2},{2,3},{3,4},{4,5},{5,6},{6,7},{8,9},{9,10},{10,11},{11... | collective-permute-start | bytes 9992 | tf_op jit(solution)/shard_map/ppermute | solution.py:41
  327.2 0.9 copy-start.5
  327.2 1.1 copy-start.6
  328.3 1.0 copy-start.3
  328.3 1.0 copy-start.4
Sparse Core Ops, SparseCore 0:
  10.9 34.0 all-reduce.1
  299.6 15.6 all-gather.1
